TPU v7x, 32 devices: a whole 2x2x4 slice. The times are simulated.
32 devices in a mesh: groups: 2 (over x), sect: 16 (over z, y, core).
Axes of the slice: x: 2, y: 2, z: 4, core: 2. Of those that a mesh axis runs over, the one named last changes fastest.
Arguments:
- psi: float32 [512, 128, 128], P(('groups', 'sect')), parts along dimension 0, may hold values from -120 to 120
- left_env: float32 [32, 32, 128, 128], P(('groups', 'sect')), parts along dimension 0, may hold values from -4 to 7
- right_env: float32 [32, 32, 128, 128], P(('groups', 'sect')), parts along dimension 0, may hold values from -4 to 7
- right_sector: int32 [512], P(('groups', 'sect')), parts along dimension 0, may hold values from 0 to 15, as said below
- mpo_pairs: int32 [64, 2], replicated, may hold values from 0 to 31
- mpo_coef: float32 [64], replicated, may hold values from 0 to 0.03125
Outputs:
- hpsi: float32 [512, 128, 128], P(('groups', 'sect')), parts along dimension 0
- residual: float32 [512, 128, 128], P(('groups', 'sect')), parts along dimension 0
There are 2 independent parts, one for each index of `groups`. A program takes and returns all parts, laid end to end along the dimension named above; an argument that names none is the same for every part. Nothing has to cross between parts.
Inputs may be any that keep to these rules, and one draw needn't show every extreme that they name: `right_sector`: the right sector of block k differs from its left sector k // 16 by at most one. Among the 16 blocks of one left sector at most 2 have right sector one higher and at most 2 one lower; some sector has exactly 2 of each, and every sector that has a higher or lower neighbour has at least one block going to it.
All inputs are finite; a program needn't handle non-finite values.
Results may differ from a plain program's by a relative error of at most 0.0003.
Values sent between devices are 32-bit elements; how exact they have to be, the bound alone decides.
A program may use at most 192 MiB of HBM per device.

v0:
```python
import jax
import jax.numpy as jnp
from jax import lax
from jax.sharding import PartitionSpec as P

CAP = 2


def passed_along(shard, axis, by):
    length = lax.axis_size(axis)
    pairs = [(i, i + by) for i in range(length) if 0 <= i + by < length]
    return lax.ppermute(shard, axis, pairs)


def on_device(psi, left_env, right_env, right_sector, mpo_pairs, mpo_coef):
    highest = lax.Precision.HIGHEST
    n_bonds = left_env.shape[1]
    bond_ids = jnp.arange(n_bonds, dtype=jnp.int32)
    left_hot = (mpo_pairs[:, 0:1] == bond_ids[None, :]).astype(jnp.float32)
    right_hot = (mpo_pairs[:, 1:2] == bond_ids[None, :]).astype(jnp.float32)
    coupling = jnp.dot(left_hot.T, right_hot * mpo_coef[:, None], precision=highest)
    offset = right_sector - lax.axis_index("sect")
    left_here = left_env[0]

    def project(block):
        proj = jnp.einsum("wij,jl->wil", left_here, block, precision=highest)
        return jnp.einsum("wv,wil->vil", coupling, proj, precision=highest)

    terms = lax.map(project, psi)
    own_env = right_env[0]
    stay = (offset == 0).astype(jnp.float32)
    hpsi = jnp.einsum("kvil,vlm->kim", terms, own_env, precision=highest) * stay[:, None, None]
    slot_ids = jnp.arange(CAP, dtype=jnp.int32)[None, :]
    going_up = offset == 1
    up_rank = jnp.cumsum(going_up.astype(jnp.int32)) - 1
    up_hot = (going_up[:, None] & (up_rank[:, None] == slot_ids)).astype(jnp.float32)
    up_send = jnp.einsum("kc,kvil->cvil", up_hot, terms, precision=highest)
    up_came = passed_along(up_send, "sect", 1)
    up_done = jnp.einsum("cvil,vlm->cim", up_came, own_env, precision=highest)
    up_back = passed_along(up_done, "sect", -1)
    hpsi = hpsi + jnp.einsum("kc,cim->kim", up_hot, up_back, precision=highest)
    going_down = offset == -1
    down_rank = jnp.cumsum(going_down.astype(jnp.int32)) - 1
    down_hot = (going_down[:, None] & (down_rank[:, None] == slot_ids)).astype(jnp.float32)
    down_send = jnp.einsum("kc,kvil->cvil", down_hot, terms, precision=highest)
    down_came = passed_along(down_send, "sect", -1)
    down_done = jnp.einsum("cvil,vlm->cim", down_came, own_env, precision=highest)
    down_back = passed_along(down_done, "sect", 1)
    hpsi = hpsi + jnp.einsum("kc,cim->kim", down_hot, down_back, precision=highest)
    totals = lax.psum((jnp.sum(psi * hpsi), jnp.sum(psi * psi)), "sect")
    energy = totals[0] / totals[1]
    return (hpsi, hpsi - energy * psi)


def solution(mesh):
    in_specs = (
        P(("groups", "sect"), None, None),
        P(("groups", "sect"), None, None, None),
        P(("groups", "sect"), None, None, None),
        P(("groups", "sect")),
        P(),
        P(),
    )
    out_specs = (P(("groups", "sect"), None, None), P(("groups", "sect"), None, None))
    return jax.shard_map(
        on_device, mesh=mesh, in_specs=in_specs, out_specs=out_specs, check_vma=False
    )
```

profile of v0, /device:TPU:0, one launch (start us, length us, event | category | flops | bytes accessed | tf_op | source)
XLA Modules:
  0.0 378.1 jit_solution(17433229510085162314)
XLA Ops:
  2.4 124.1 %while.10 = (s32[]{:T(128)}, f32[16,32,128,128]{3,1,2,0:T(8,128)}, f32[16,128,128]{2,1,0:T(8,128)}, f32[32,128,128]{2,1,0:T(8,128)}, f32[32,32]{0,1:T(8,128)S(1)}, /*index=5*/s32[]{:T(128)}) while((s32[]{:T(128)}, f32[16,32,128,128]{3,1,2,0:T(8,128)}, f32[16,128,128]{2,1,0:T(8,128)}, f32[32,128,128]{2,1,0:T(8,128)}, f32[32,32]{0,1:T(8,128)S(1)}, ...), condition=%wide.region_1.2_spmd, body=%wide.region_0.1_spmd.sunk | while | flops 1006632960 | bytes 8458325 | solution.py:29
  2.5 4.5 %fusion.69 = f32[128,32,128]{0,1,2:T(8,128)S(1)} fusion(f32[32,128,128]{2,1,0:T(8,128)} %get-tuple-element.110, f32[16,128,128]{2,1,0:T(8,128)} %get-tuple-element.109, s32[]{:T(128)S(6)} %copy.59), kind=kOutput, calls=%fused_computation.3.clone.1 | convolution fusion | flops 805306368 | bytes 4259844 | tf_op jit(solution)/shard_map/while/body/eval_jaxpr/wij,jl->wil/dot_general | solution.py:26
  7.0 3.2 bitcast_dynamic-update-slice_fusion.2
  10.2 4.5 %fusion.69 = f32[128,32,128]{0,1,2:T(8,128)S(1)} fusion(f32[32,128,128]{2,1,0:T(8,128)} %get-tuple-element.110, f32[16,128,128]{2,1,0:T(8,128)} %get-tuple-element.109, s32[]{:T(128)S(6)} %copy.59), kind=kOutput, calls=%fused_computation.3.clone.1 | convolution fusion | flops 805306368 | bytes 4259844 | tf_op jit(solution)/shard_map/while/body/eval_jaxpr/wij,jl->wil/dot_general | solution.py:26
  18.0 4.5 %fusion.69 = f32[128,32,128]{0,1,2:T(8,128)S(1)} fusion(f32[32,128,128]{2,1,0:T(8,128)} %get-tuple-element.110, f32[16,128,128]{2,1,0:T(8,128)} %get-tuple-element.109, s32[]{:T(128)S(6)} %copy.59), kind=kOutput, calls=%fused_computation.3.clone.1 | convolution fusion | flops 805306368 | bytes 4259844 | tf_op jit(solution)/shard_map/while/body/eval_jaxpr/wij,jl->wil/dot_general | solution.py:26
  25.7 4.5 %fusion.69 = f32[128,32,128]{0,1,2:T(8,128)S(1)} fusion(f32[32,128,128]{2,1,0:T(8,128)} %get-tuple-element.110, f32[16,128,128]{2,1,0:T(8,128)} %get-tuple-element.109, s32[]{:T(128)S(6)} %copy.59), kind=kOutput, calls=%fused_computation.3.clone.1 | convolution fusion | flops 805306368 | bytes 4259844 | tf_op jit(solution)/shard_map/while/body/eval_jaxpr/wij,jl->wil/dot_general | solution.py:26
  33.5 4.5 %fusion.69 = f32[128,32,128]{0,1,2:T(8,128)S(1)} fusion(f32[32,128,128]{2,1,0:T(8,128)} %get-tuple-element.110, f32[16,128,128]{2,1,0:T(8,128)} %get-tuple-element.109, s32[]{:T(128)S(6)} %copy.59), kind=kOutput, calls=%fused_computation.3.clone.1 | convolution fusion | flops 805306368 | bytes 4259844 | tf_op jit(solution)/shard_map/while/body/eval_jaxpr/wij,jl->wil/dot_general | solution.py:26
  38.0 3.3 bitcast_dynamic-update-slice_fusion.2
  41.3 4.5 %fusion.69 = f32[128,32,128]{0,1,2:T(8,128)S(1)} fusion(f32[32,128,128]{2,1,0:T(8,128)} %get-tuple-element.110, f32[16,128,128]{2,1,0:T(8,128)} %get-tuple-element.109, s32[]{:T(128)S(6)} %copy.59), kind=kOutput, calls=%fused_computation.3.clone.1 | convolution fusion | flops 805306368 | bytes 4259844 | tf_op jit(solution)/shard_map/while/body/eval_jaxpr/wij,jl->wil/dot_general | solution.py:26
  49.0 4.5 %fusion.69 = f32[128,32,128]{0,1,2:T(8,128)S(1)} fusion(f32[32,128,128]{2,1,0:T(8,128)} %get-tuple-element.110, f32[16,128,128]{2,1,0:T(8,128)} %get-tuple-element.109, s32[]{:T(128)S(6)} %copy.59), kind=kOutput, calls=%fused_computation.3.clone.1 | convolution fusion | flops 805306368 | bytes 4259844 | tf_op jit(solution)/shard_map/while/body/eval_jaxpr/wij,jl->wil/dot_general | solution.py:26
  53.5 3.3 bitcast_dynamic-update-slice_fusion.2
  56.8 4.5 %fusion.69 = f32[128,32,128]{0,1,2:T(8,128)S(1)} fusion(f32[32,128,128]{2,1,0:T(8,128)} %get-tuple-element.110, f32[16,128,128]{2,1,0:T(8,128)} %get-tuple-element.109, s32[]{:T(128)S(6)} %copy.59), kind=kOutput, calls=%fused_computation.3.clone.1 | convolution fusion | flops 805306368 | bytes 4259844 | tf_op jit(solution)/shard_map/while/body/eval_jaxpr/wij,jl->wil/dot_general | solution.py:26
  64.5 4.5 %fusion.69 = f32[128,32,128]{0,1,2:T(8,128)S(1)} fusion(f32[32,128,128]{2,1,0:T(8,128)} %get-tuple-element.110, f32[16,128,128]{2,1,0:T(8,128)} %get-tuple-element.109, s32[]{:T(128)S(6)} %copy.59), kind=kOutput, calls=%fused_computation.3.clone.1 | convolution fusion | flops 805306368 | bytes 4259844 | tf_op jit(solution)/shard_map/while/body/eval_jaxpr/wij,jl->wil/dot_general | solution.py:26
  72.3 4.5 %fusion.69 = f32[128,32,128]{0,1,2:T(8,128)S(1)} fusion(f32[32,128,128]{2,1,0:T(8,128)} %get-tuple-element.110, f32[16,128,128]{2,1,0:T(8,128)} %get-tuple-element.109, s32[]{:T(128)S(6)} %copy.59), kind=kOutput, calls=%fused_computation.3.clone.1 | convolution fusion | flops 805306368 | bytes 4259844 | tf_op jit(solution)/shard_map/while/body/eval_jaxpr/wij,jl->wil/dot_general | solution.py:26
  80.0 4.5 %fusion.69 = f32[128,32,128]{0,1,2:T(8,128)S(1)} fusion(f32[32,128,128]{2,1,0:T(8,128)} %get-tuple-element.110, f32[16,128,128]{2,1,0:T(8,128)} %get-tuple-element.109, s32[]{:T(128)S(6)} %copy.59), kind=kOutput, calls=%fused_computation.3.clone.1 | convolution fusion | flops 805306368 | bytes 4259844 | tf_op jit(solution)/shard_map/while/body/eval_jaxpr/wij,jl->wil/dot_general | solution.py:26
  87.8 4.5 %fusion.69 = f32[128,32,128]{0,1,2:T(8,128)S(1)} fusion(f32[32,128,128]{2,1,0:T(8,128)} %get-tuple-element.110, f32[16,128,128]{2,1,0:T(8,128)} %get-tuple-element.109, s32[]{:T(128)S(6)} %copy.59), kind=kOutput, calls=%fused_computation.3.clone.1 | convolution fusion | flops 805306368 | bytes 4259844 | tf_op jit(solution)/shard_map/while/body/eval_jaxpr/wij,jl->wil/dot_general | solution.py:26
  95.5 4.5 %fusion.69 = f32[128,32,128]{0,1,2:T(8,128)S(1)} fusion(f32[32,128,128]{2,1,0:T(8,128)} %get-tuple-element.110, f32[16,128,128]{2,1,0:T(8,128)} %get-tuple-element.109, s32[]{:T(128)S(6)} %copy.59), kind=kOutput, calls=%fused_computation.3.clone.1 | convolution fusion | flops 805306368 | bytes 4259844 | tf_op jit(solution)/shard_map/while/body/eval_jaxpr/wij,jl->wil/dot_general | solution.py:26
  100.1 3.3 bitcast_dynamic-update-slice_fusion.2
  103.3 4.5 %fusion.69 = f32[128,32,128]{0,1,2:T(8,128)S(1)} fusion(f32[32,128,128]{2,1,0:T(8,128)} %get-tuple-element.110, f32[16,128,128]{2,1,0:T(8,128)} %get-tuple-element.109, s32[]{:T(128)S(6)} %copy.59), kind=kOutput, calls=%fused_computation.3.clone.1 | convolution fusion | flops 805306368 | bytes 4259844 | tf_op jit(solution)/shard_map/while/body/eval_jaxpr/wij,jl->wil/dot_general | solution.py:26
  111.1 4.5 %fusion.69 = f32[128,32,128]{0,1,2:T(8,128)S(1)} fusion(f32[32,128,128]{2,1,0:T(8,128)} %get-tuple-element.110, f32[16,128,128]{2,1,0:T(8,128)} %get-tuple-element.109, s32[]{:T(128)S(6)} %copy.59), kind=kOutput, calls=%fused_computation.3.clone.1 | convolution fusion | flops 805306368 | bytes 4259844 | tf_op jit(solution)/shard_map/while/body/eval_jaxpr/wij,jl->wil/dot_general | solution.py:26
  115.6 3.2 bitcast_dynamic-update-slice_fusion.2
  118.8 4.5 %fusion.69 = f32[128,32,128]{0,1,2:T(8,128)S(1)} fusion(f32[32,128,128]{2,1,0:T(8,128)} %get-tuple-element.110, f32[16,128,128]{2,1,0:T(8,128)} %get-tuple-element.109, s32[]{:T(128)S(6)} %copy.59), kind=kOutput, calls=%fused_computation.3.clone.1 | convolution fusion | flops 805306368 | bytes 4259844 | tf_op jit(solution)/shard_map/while/body/eval_jaxpr/wij,jl->wil/dot_general | solution.py:26
  126.8 46.4 %fusion.12 = f32[2,32,128,128]{3,0,2,1:T(2,128)} fusion(f32[16,32,128,128]{3,1,2,0:T(8,128)} %get-tuple-element.29, pred[16]{0:T(512)(128)(4,1)S(1)} %get-tuple-element.62, s32[16]{0:T(128)S(1)} %add_reduce_fusion), kind=kOutput, calls=%fused_computation.11 | convolution fusion | flops 201326656 | bytes 37748816 | tf_op jit(solution)/shard_map/kc,kvil->cvil/dot_general | solution.py:45
  173.2 4.8 %copy.28 = f32[2,32,128,128]{3,2,1,0:T(8,128)} copy(f32[2,32,128,128]{3,0,2,1:T(2,128)} %fusion.12) | data formatting | bytes 8388608 | tf_op jit(solution)/shard_map/kc,kvil->cvil/dot_general | solution.py:45
  179.5 46.7 %fusion.14 = f32[2,32,128,128]{3,0,2,1:T(2,128)} fusion(f32[16,32,128,128]{3,1,2,0:T(8,128)} %get-tuple-element.29, pred[16]{0:T(512)(128)(4,1)S(1)} %get-tuple-element.55, s32[16]{0:T(128)S(1)} %add_reduce_fusion.1), kind=kOutput, calls=%fused_computation.13 | convolution fusion | flops 201326656 | bytes 37748816 | tf_op jit(solution)/shard_map/kc,kvil->cvil/dot_general | solution.py:37
  229.0 3.3 collective-permute-start
  232.3 5.9 %fusion.16 = f32[2,128,128,1]{2,1,3,0:T(8,128)S(1)} fusion(f32[2,32,128,128]{3,2,1,0:T(8,128)} %collective-permute-done.2, f32[1,32,128,128]{3,2,1,0:T(8,128)S(1)} %copy-done), kind=kOutput, calls=%fused_computation.15 | convolution fusion | flops 1610612736 | bytes 6422528 | tf_op jit(solution)/shard_map/cvil,vlm->cim/dot_general | solution.py:47
  238.4 4.4 %collective-permute-start.3 = (f32[2,128,128]{2,0,1:T(2,128)S(1)}, f32[2,128,128]{2,0,1:T(2,128)S(1)}, u32[]{:S(2)}, u32[]{:S(2)}) collective-permute-start(f32[2,128,128]{2,0,1:T(2,128)S(1)} %bitcast.83), channel_id=1, source_target_pairs={{0,1},{1,2},{2,3},{3,4},{4,5},{5,6},{6,7},{7,8},{8,9},{9,10},{10,1... | collective-permute-start | bytes 393224 | tf_op jit(solution)/shard_map/ppermute | solution.py:12
  242.8 3.5 fusion.18
  248.3 38.1 %collective-permute-done.1 = f32[2,128,128]{2,0,1:T(2,128)S(1)} collective-permute-done((f32[2,128,128]{2,0,1:T(2,128)S(1)}, f32[2,128,128]{2,0,1:T(2,128)S(1)}, u32[]{:S(2)}, u32[]{:S(2)}) %collective-permute-start.1) | collective-permute-done | bytes 131104 | tf_op jit(solution)/shard_map/ppermute | solution.py:12
  287.1 51.3 %multiply_reduce_fusion = (f32[]{:T(128)}, f32[]{:T(128)}, f32[16,128,128]{2,1,0:T(8,128)}) fusion(f32[16,128,128]{2,1,0:T(8,128)S(1)} %copy-done.1, f32[16,128,128]{2,0,1:T(8,128)S(1)} %fusion.43, f32[16,128,128]{2,0,1:T(8,128)S(1)} %fusion.45, f32[16]{0:T(128)S(1)} %get-tuple-element.60, f32[1,32,128,128]{3,2,1,0:T(8,128)S(1)} %copy-done, ...), kind=kOutput, calls=%fused_computation.25 | convolution fusion | flops 12886736896 | bytes 39845960 | tf_op jit(solution)/shard_map/kvil,vlm->kim/dot_general | solution.py:32
  338.4 35.8 %all-reduce = (f32[]{:T(128)}, f32[]{:T(128)}) all-reduce(f32[]{:T(128)} %get-tuple-element.41, f32[]{:T(128)} %get-tuple-element.40), channel_id=1, replica_groups=mesh['groups'=2,'sect'=16] {'sect'}, use_global_device_ids=true, to_apply=%region_5.6 | all-reduce | flops 2 | bytes 16 | tf_op jit(solution)/shard_map/psum | solution.py:50
  (38 shorter events, 46.8 us)
Async XLA Ops:
  0.6 231.7 %copy-start = (f32[1,32,128,128]{3,2,1,0:T(8,128)S(1)}, f32[1,32,128,128]{3,2,1,0:T(8,128)}, u32[]{:S(2)}) copy-start(f32[1,32,128,128]{3,2,1,0:T(8,128)} %param.10) | copy-start | bytes 6291460
  2.4 124.1 %copy-start.2 = (s32[16]{0:T(128)S(1)}, s32[16]{0:T(128)}, u32[]{:S(2)}) copy-start(s32[16]{0:T(128)} %param.11) | copy-start | bytes 196
  178.0 54.3 %collective-permute-start.2 = (f32[2,32,128,128]{3,2,1,0:T(8,128)}, f32[2,32,128,128]{3,2,1,0:T(8,128)}, u32[]{:S(2)}, u32[]{:S(2)}) collective-permute-start(f32[2,32,128,128]{3,2,1,0:T(8,128)} %copy.28), channel_id=1, source_target_pairs={{1,0},{2,1},{3,2},{4,3},{5,4},{6,5},{7,6},{8,7},{9,8},{10,9},{11,1... | collective-permute-start | bytes 12582920 | tf_op jit(solution)/shard_map/ppermute | solution.py:12
  229.0 13.8 %collective-permute-start = (f32[2,32,128,128]{3,2,1,0:T(8,128)S(1)}, f32[2,32,128,128]{3,2,1,0:T(8,128)S(1)}, u32[]{:S(2)}, u32[]{:S(2)}) collective-permute-start(f32[2,32,128,128]{3,2,1,0:T(8,128)S(1)} %copy.25), channel_id=1, source_target_pairs={{0,1},{1,2},{2,3},{3,4},{4,5},{5,6},{6,7},{7,8},{8,9},{9,10},{10,1... | collective-permute-start | bytes 12582920 | tf_op jit(solution)/shard_map/ppermute | solution.py:12
  238.4 48.7 %copy-start.1 = (f32[16,128,128]{2,1,0:T(8,128)S(1)}, f32[16,128,128]{2,1,0:T(8,128)}, u32[]{:S(2)}) copy-start(f32[16,128,128]{2,1,0:T(8,128)} %get-tuple-element.113) | copy-start | bytes 3145732
  238.4 9.3 %collective-permute-start.3 = (f32[2,128,128]{2,0,1:T(2,128)S(1)}, f32[2,128,128]{2,0,1:T(2,128)S(1)}, u32[]{:S(2)}, u32[]{:S(2)}) collective-permute-start(f32[2,128,128]{2,0,1:T(2,128)S(1)} %bitcast.83), channel_id=1, source_target_pairs={{0,1},{1,2},{2,3},{3,4},{4,5},{5,6},{6,7},{7,8},{8,9},{9,10},{10,1... | collective-permute-start | bytes 393224 | tf_op jit(solution)/shard_map/ppermute | solution.py:12
  246.4 40.0 %collective-permute-start.1 = (f32[2,128,128]{2,0,1:T(2,128)S(1)}, f32[2,128,128]{2,0,1:T(2,128)S(1)}, u32[]{:S(2)}, u32[]{:S(2)}) collective-permute-start(f32[2,128,128]{2,0,1:T(2,128)S(1)} %bitcast.84), channel_id=1, source_target_pairs={{1,0},{2,1},{3,2},{4,3},{5,4},{6,5},{7,6},{8,7},{9,8},{10,9},{11,1... | collective-permute-start | bytes 393224 | tf_op jit(solution)/shard_map/ppermute | solution.py:12
where the time goes:
time: 383 us; the launch traced here: 378 us
  matrix products  280 us (73%)
  waiting for transfers between devices  38.1 us (10%)
  blocking collectives  35.8 us (9%)
  starting transfers between devices  10.2 us (3%)
  local copies, waits for them, and re-layouts  8.79 us (2%)
    dot_general x16, matrix products, project(): proj = jnp.einsum('wij,jl->wil', left_here, block, precision=highest)  72.3 us
    dot_general x16, matrix products, project(): return jnp.einsum('wv,wil->vil', coupling, proj, precision=highest)  51.7 us
    dot_general x1, matrix products, on_device(): jnp.einsum('kvil,vlm->kim', terms, own_env, precision=highest)  51.3 us
    dot_general x1, matrix products, on_device(): up_send = jnp.einsum('kc,kvil->cvil', up_hot, terms, precision=highest)  46.7 us
    dot_general x1, matrix products, on_device(): down_send = jnp.einsum('kc,kvil->cvil', down_hot, terms, precision=highest)  46.4 us
    ppermute x4, waiting for transfers between devices, passed_along(): return lax.ppermute(shard, axis, pairs)  38.1 us
    psum x1, blocking collectives, on_device(): totals = lax.psum((jnp.sum(psi * hpsi), jnp.sum(psi * psi)), 'sect')  35.8 us
    ppermute x4, starting transfers between devices, passed_along(): return lax.ppermute(shard, axis, pairs)  10.2 us
  transfers between devices with their start and end apart: 4, of which 1 were waited for; matrix products, arithmetic and copies ran while one was open for 16% of the time, Pallas kernels for 0%

commit v1 on v0

v1 whole, which is shorter than its diff:
```python
import functools
import jax
import jax.numpy as jnp
from jax import lax
from jax.experimental import pallas as pl
from jax.experimental.pallas import tpu as pltpu
from jax.sharding import PartitionSpec as P

CAP = 2
F32 = jnp.float32
BF16 = jnp.bfloat16


def split(x):
    hi = x.astype(BF16)
    return hi, (x - hi.astype(F32)).astype(BF16)


def dot(a, b):
    return jnp.dot(a, b, preferred_element_type=F32)


def kernel(
    n, vc,
    psi_in, left_in, right_in, sector, pairs, coef,
    hpsi_out, res_out,
    psi, left, right, r_hi, r_lo, m_cat, p_cat, r_cat, t_hi, t_lo, off_hi, off_lo,
    acc, hp, res, c_vec, c_sm, part, parts,
    local_sem, up_send, up_recv, dn_send, dn_recv, part_send, part_recv,
):
    nk, bs, _ = psi.shape
    nv = left.shape[0]
    nq = nv // vc
    wide = vc * bs
    me = lax.axis_index("sect")

    loads = [
        pltpu.make_async_copy(left_in.at[0], left, local_sem.at[0]),
        pltpu.make_async_copy(psi_in, psi, local_sem.at[1]),
        pltpu.make_async_copy(right_in.at[0], right, local_sem.at[2]),
    ]
    for c in loads:
        c.start()

    barrier = pltpu.get_barrier_semaphore()

    def greet(d, carry):
        pl.semaphore_signal(
            barrier, inc=1, device_id={"sect": lax.rem(me + d, n)}, device_id_type=pl.DeviceIdType.MESH
        )
        return carry

    lax.fori_loop(1, n, greet, 0)
    pl.semaphore_wait(barrier, n - 1)

    def up_copy(q):
        at = pl.ds(q * vc, vc)
        return pltpu.make_async_remote_copy(
            src_ref=right_in.at[0, at], dst_ref=r_lo.at[at],
            send_sem=up_send.at[q], recv_sem=up_recv.at[q],
            device_id={"sect": me + 1}, device_id_type=pl.DeviceIdType.MESH,
        )

    def dn_copy(q):
        at = pl.ds(q * vc, vc)
        return pltpu.make_async_remote_copy(
            src_ref=right_in.at[0, at], dst_ref=r_hi.at[at],
            send_sem=dn_send.at[q], recv_sem=dn_recv.at[q],
            device_id={"sect": me - 1}, device_id_type=pl.DeviceIdType.MESH,
        )

    has_up = me < n - 1
    has_dn = me > 0
    for q in range(nq):
        @pl.when(has_up)
        def _():
            up_copy(q).start()

        @pl.when(has_dn)
        def _():
            dn_copy(q).start()

    zero = jnp.int32(0)
    picks = [zero] * (2 * CAP)
    n_up = zero
    n_dn = zero
    slots = []
    for k in range(nk):
        offset = sector[k] - me
        up = offset == 1
        dn = offset == -1
        for c in range(CAP):
            picks[c] = jnp.where(up & (n_up == c), k, picks[c])
            picks[CAP + c] = jnp.where(dn & (n_dn == c), k, picks[CAP + c])
        slots.append(jnp.where(up, nk + jnp.minimum(n_up, CAP - 1), jnp.where(dn, nk + CAP + jnp.minimum(n_dn, CAP - 1), k)))
        n_up = n_up + up.astype(jnp.int32)
        n_dn = n_dn + dn.astype(jnp.int32)

    ids = lax.broadcasted_iota(jnp.int32, (pairs.shape[0], 128), 1)
    left_hot = (pairs[:, 0:1] == ids).astype(F32)
    right_hot = jnp.where(pairs[:, 1:2] == ids, coef[...], 0.0)
    coupling = lax.dot_general(
        right_hot, left_hot, (((0,), (0,)), ((), ())),
        precision=lax.Precision.HIGHEST, preferred_element_type=F32,
    )
    c_vec[...] = coupling[:nv]
    c_copy = pltpu.make_async_copy(c_vec, c_sm, local_sem.at[5])
    c_copy.start()
    c_copy.wait()

    acc[...] = jnp.zeros_like(acc)

    loads[0].wait()

    def mix(u, carry):
        total = c_sm[u, 0] * left[0]
        for w in range(1, nv):
            total = total + c_sm[u, w] * left[w]
        hi, lo = split(total)
        m_cat[u, :, 0:bs] = hi
        m_cat[u, :, bs:2 * bs] = lo
        m_cat[u, :, 2 * bs:] = hi
        return carry

    lax.fori_loop(0, nv, mix, 0)

    loads[1].wait()

    def pack_psi(kp, carry):
        for s in range(2):
            hi, lo = split(psi[2 * kp + s])
            lanes = slice(s * bs, (s + 1) * bs)
            p_cat[kp, 0:bs, lanes] = hi
            p_cat[kp, bs:2 * bs, lanes] = hi
            p_cat[kp, 2 * bs:, lanes] = lo
        return carry

    lax.fori_loop(0, nk // 2, pack_psi, 0)
    loads[2].wait()

    def pack_right(u, carry):
        hi, lo = split(right[u])
        r_cat[u, :, 0:bs] = hi
        r_cat[u, :, bs:] = lo
        return carry

    lax.fori_loop(0, nv, pack_right, 0)

    half = nk // 2

    def own(q, carry):
        lhs = m_cat[pl.ds(q * vc, vc)].reshape(wide, 3 * bs)

        def terms(kp, carry):
            hi, lo = split(dot(lhs, p_cat[kp]))
            for v in range(vc):
                rows = slice(v * bs, (v + 1) * bs)
                for s in range(2):
                    lanes = slice(s * bs, (s + 1) * bs)
                    t_hi[2 * kp + s, :, rows] = hi[rows, lanes]
                    t_lo[2 * kp + s, :, rows] = lo[rows, lanes]
            return carry

        lax.fori_loop(0, nk // 2, terms, 0)
        for c in range(2 * CAP):
            off_hi[q, c] = t_hi[picks[c]]
            off_lo[q, c] = t_lo[picks[c]]

        rhs = r_cat[pl.ds(q * vc, vc)].reshape(wide, 2 * bs)

        def close(g, carry):
            at = pl.ds(g * half, half)
            d = dot(t_hi[at].reshape(half * bs, wide), rhs)
            e = dot(t_lo[at].reshape(half * bs, wide), rhs[:, :bs])
            acc[at] += (d[:, :bs] + d[:, bs:] + e).reshape(half, bs, bs)
            return carry

        lax.fori_loop(0, 2, close, 0)
        return carry

    lax.fori_loop(0, nq, own, 0)

    def away(q, carry):
        at = pl.ds(q * vc, vc)

        def add(came, first):
            hi, lo = split(came[at].reshape(wide, bs))
            rows = slice(first, first + CAP)
            a = off_hi[q, rows].reshape(CAP * bs, wide)
            b = off_lo[q, rows].reshape(CAP * bs, wide)
            total = dot(a, hi) + dot(a, lo) + dot(b, hi)
            acc[nk + first:nk + first + CAP] += total.reshape(CAP, bs, bs)

        @pl.when(has_dn)
        def _():
            up_copy(q).wait_recv()
            add(r_lo, CAP)

        @pl.when(has_up)
        def _():
            dn_copy(q).wait_recv()
            add(r_hi, 0)

        return carry

    lax.fori_loop(0, nq, away, 0)

    s1 = jnp.zeros((8, bs), F32)
    s2 = jnp.zeros((8, bs), F32)
    for k in range(nk):
        product = acc[slots[k]]
        block = psi[k]
        hp[k] = product
        s1 = s1 + jnp.sum((block * product).reshape(bs // 8, 8, bs), axis=0)
        s2 = s2 + jnp.sum((block * block).reshape(bs // 8, 8, bs), axis=0)
    part[0:8] = s1
    part[8:16] = s2

    def part_copy(d):
        return pltpu.make_async_remote_copy(
            src_ref=part, dst_ref=parts.at[d],
            send_sem=part_send.at[d], recv_sem=part_recv.at[d],
            device_id={"sect": lax.rem(me + d, n)}, device_id_type=pl.DeviceIdType.MESH,
        )

    def tell(d, carry):
        part_copy(d).start()
        return carry

    lax.fori_loop(1, n, tell, 0)
    hp_copy = pltpu.make_async_copy(hp, hpsi_out, local_sem.at[3])
    hp_copy.start()

    def hear(d, total):
        part_copy(d).wait_recv()
        return total + parts[d]

    total = lax.fori_loop(1, n, hear, part[...])
    energy = jnp.sum(total[0:8], keepdims=True) / jnp.sum(total[8:16], keepdims=True)
    for k in range(nk):
        res[k] = hp[k] - energy * psi[k]
    res_copy = pltpu.make_async_copy(res, res_out, local_sem.at[4])
    res_copy.start()

    def sent(d, carry):
        part_copy(d).wait_send()
        return carry

    lax.fori_loop(1, n, sent, 0)
    for q in range(nq):
        @pl.when(has_up)
        def _():
            up_copy(q).wait_send()

        @pl.when(has_dn)
        def _():
            dn_copy(q).wait_send()

    hp_copy.wait()
    res_copy.wait()


def on_device(n, psi, left_env, right_env, right_sector, mpo_pairs, mpo_coef):
    nk, bs, _ = psi.shape
    nv = left_env.shape[1]
    vc = 8 if nv % 8 == 0 else nv
    nq = nv // vc
    vmem = pltpu.VMEM
    dma = pltpu.SemaphoreType.DMA
    anywhere = pl.BlockSpec(memory_space=pl.ANY)
    return pl.pallas_call(
        functools.partial(kernel, n, vc),
        out_shape=(jax.ShapeDtypeStruct(psi.shape, F32), jax.ShapeDtypeStruct(psi.shape, F32)),
        in_specs=[
            anywhere, anywhere, anywhere,
            pl.BlockSpec(memory_space=pltpu.SMEM),
            pl.BlockSpec(memory_space=vmem),
            pl.BlockSpec(memory_space=vmem),
        ],
        out_specs=(anywhere, anywhere),
        scratch_shapes=[
            vmem((nk, bs, bs), F32),
            vmem((nv, bs, bs), F32),
            vmem((nv, bs, bs), F32),
            vmem((nv, bs, bs), F32),
            vmem((nv, bs, bs), F32),
            vmem((nv, bs, 3 * bs), BF16),
            vmem((nk // 2, 3 * bs, 2 * bs), BF16),
            vmem((nv, bs, 2 * bs), BF16),
            vmem((nk, bs, vc * bs), BF16),
            vmem((nk, bs, vc * bs), BF16),
            vmem((nq, 2 * CAP, bs, vc * bs), BF16),
            vmem((nq, 2 * CAP, bs, vc * bs), BF16),
            vmem((nk + 2 * CAP, bs, bs), F32),
            vmem((nk, bs, bs), F32),
            vmem((nk, bs, bs), F32),
            vmem((nv, 128), F32),
            pltpu.SMEM((nv, 128), F32),
            vmem((16, bs), F32),
            vmem((n, 16, bs), F32),
            dma((6,)),
            dma((nq,)), dma((nq,)), dma((nq,)), dma((nq,)),
            dma((n,)), dma((n,)),
        ],
        compiler_params=pltpu.CompilerParams(
            collective_id=0, has_side_effects=True, vmem_limit_bytes=56 * 1024 * 1024
        ),
    )(psi, left_env, right_env, right_sector, mpo_pairs, mpo_coef[:, None])


def solution(mesh):
    in_specs = (
        P(("groups", "sect"), None, None),
        P(("groups", "sect"), None, None, None),
        P(("groups", "sect"), None, None, None),
        P(("groups", "sect")),
        P(),
        P(),
    )
    out_specs = (P(("groups", "sect"), None, None), P(("groups", "sect"), None, None))
    return jax.shard_map(
        functools.partial(on_device, mesh.shape["sect"]),
        mesh=mesh, in_specs=in_specs, out_specs=out_specs, check_vma=False,
    )
```

time: 383 us -> 67.9 us (0.18); the launches traced: 378 us -> 67.6 us
  matrix products: 280 us -> 0 us
  Pallas kernels: 0 us -> 60.9 us
  waiting for transfers between devices: 38.1 us -> 0 us
  blocking collectives: 35.8 us -> 0 us
  starting transfers between devices: 10.2 us -> 0 us
    dot_general x40 -> x0, matrix products: 280 us -> none  [the longest x16 72.3 us: project(): proj = jnp.einsum('wij,jl->wil', left_here, block, precision=highest)]
    pallas_call x0 -> x1, Pallas kernels: none -> 60.9 us  [on_device(): pl.pallas_call(functools.partial(kernel, n, vc), out_shape=(jax.ShapeDtyp...]
    ppermute x4 -> x0, waiting for transfers between devices: 38.1 us -> none  [passed_along(): return lax.ppermute(shard, axis, pairs)]
    psum x1 -> x0, blocking collectives: 35.8 us -> none  [on_device(): totals = lax.psum((jnp.sum(psi * hpsi), jnp.sum(psi * psi)), 'sect')]
    ppermute x4 -> x0, starting transfers between devices: 10.2 us -> none  [passed_along(): return lax.ppermute(shard, axis, pairs)]
    dot_general x4 -> x0, local copies, waits for them, and re-layouts: 7.75 us -> none  [the longest x1 4.8 us: on_device(): down_send = jnp.einsum('kc,kvil->cvil', down_hot, terms, precision=highest)]
    unnamed x6 -> x5, local copies, waits for them, and re-layouts: 0.02 us -> 4.74 us
  transfers between devices with their start and end apart: 4 -> 0, of which waited for: 1 -> 0; matrix products, arithmetic and copies ran while one was open for 16% -> 0% of each run, Pallas kernels for 0% -> 0%
where the time goes in v1:
time: 67.9 us; the launch traced here: 67.6 us
  Pallas kernels  60.9 us (90%)
  local copies, waits for them, and re-layouts  6.1 us (9%)
    pallas_call x1, Pallas kernels, on_device(): pl.pallas_call(functools.partial(kernel, n, vc), out_shape=(jax.ShapeDtyp...  60.9 us
    unnamed x5, local copies, waits for them, and re-layouts  4.74 us

profile of v1, /device:TPU:0, one launch (start us, length us, event | category | flops | bytes accessed | tf_op | source)
XLA Modules:
  0.0 67.6 jit_solution(8428305212891641932)
XLA Ops:
  0.6 1.4 %copy.8.pairs = s32[64,2]{1,0:T(8,128)} copy(s32[64,2]{0,1:T(2,128)} %param.10) | data formatting | bytes 1024 | tf_op args[4]
  2.0 1.4 %copy.9.coef = f32[64,1]{1,0:T(8,128)} copy(f32[64,1]{0,1:T(1,128)} %bitcast.1) | data formatting | bytes 512 | tf_op jit(solution)/shard_map/broadcast_in_dim | solution.py:308
  3.4 60.9 %shard_map.77 = (f32[16,128,128]{2,1,0:T(8,128)}, f32[16,128,128]{2,1,0:T(8,128)}) custom-call(f32[16,128,128]{2,1,0:T(8,128)} %psi_in.1, f32[1,32,128,128]{3,2,1,0:T(8,128)} %left_in.1, f32[1,32,128,128]{3,2,1,0:T(8,128)} %right_in.1, s32[16]{0:T(128)} %sector.1, s32[64,2]{1,0:T(8,128)} %copy.8.pairs, f32[64,1]{1,0:T(8,128)} %copy.9.coef), custom_call_target="tpu_custom_call" | custom-call | tf_op jit(solution)/shard_map/pallas_call | solution.py:271
  64.3 0.0 copy-start
  64.3 2.4 %copy.12 = f32[16,128,128]{2,1,0:T(8,128)} copy(f32[16,128,128]{2,1,0:T(8,128)} %get-tuple-element.4) | data formatting | bytes 2097152
  66.7 0.0 copy-done
  66.7 1.0 %copy.13 = f32[16,128,128]{2,1,0:T(8,128)} copy(f32[16,128,128]{2,1,0:T(8,128)S(1)} %copy-done) | data formatting | bytes 2097152
Async XLA Ops:
  64.3 2.4 %copy-start = (f32[16,128,128]{2,1,0:T(8,128)S(1)}, f32[16,128,128]{2,1,0:T(8,128)}, u32[]{:S(2)}) copy-start(f32[16,128,128]{2,1,0:T(8,128)} %get-tuple-element.5) | copy-start | bytes 3145732

commit v2 on v1

--- a/solution.py
+++ b/solution.py
@@ -21,17 +21,20 @@
 
 
 def kernel(
-    n, vc,
+    n, vc, xc,
     psi_in, left_in, right_in, sector, pairs, coef,
-    hpsi_out, res_out,
+    hpsi_out, energy_out,
     psi, left, right, r_hi, r_lo, m_cat, p_cat, r_cat, t_hi, t_lo, off_hi, off_lo,
-    acc, hp, res, c_vec, c_sm, part, parts,
+    acc, hp, c_vec, c_sm, part, parts,
     local_sem, up_send, up_recv, dn_send, dn_recv, part_send, part_recv,
 ):
     nk, bs, _ = psi.shape
     nv = left.shape[0]
     nq = nv // vc
+    nx = nv // xc
+    per = vc // xc
     wide = vc * bs
+    narrow = xc * bs
     me = lax.axis_index("sect")
 
     loads = [
@@ -54,7 +57,7 @@
     pl.semaphore_wait(barrier, n - 1)
 
     def up_copy(q):
-        at = pl.ds(q * vc, vc)
+        at = pl.ds(q * xc, xc)
         return pltpu.make_async_remote_copy(
             src_ref=right_in.at[0, at], dst_ref=r_lo.at[at],
             send_sem=up_send.at[q], recv_sem=up_recv.at[q],
@@ -62,7 +65,7 @@
         )
 
     def dn_copy(q):
-        at = pl.ds(q * vc, vc)
+        at = pl.ds(q * xc, xc)
         return pltpu.make_async_remote_copy(
             src_ref=right_in.at[0, at], dst_ref=r_hi.at[at],
             send_sem=dn_send.at[q], recv_sem=dn_recv.at[q],
@@ -71,7 +74,8 @@
 
     has_up = me < n - 1
     has_dn = me > 0
-    for q in range(nq):
+    from_up, from_dn = has_up, has_dn
+    for q in range(nx):
         @pl.when(has_up)
         def _():
             up_copy(q).start()
@@ -96,11 +100,11 @@
         n_up = n_up + up.astype(jnp.int32)
         n_dn = n_dn + dn.astype(jnp.int32)
 
-    ids = lax.broadcasted_iota(jnp.int32, (pairs.shape[0], 128), 1)
-    left_hot = (pairs[:, 0:1] == ids).astype(F32)
-    right_hot = jnp.where(pairs[:, 1:2] == ids, coef[...], 0.0)
+    ids = lax.broadcasted_iota(jnp.int32, (128, pairs.shape[1]), 0)
+    left_hot = (pairs[0:1, :] == ids).astype(F32)
+    right_hot = jnp.where(pairs[1:2, :] == ids, coef[...], 0.0)
     coupling = lax.dot_general(
-        right_hot, left_hot, (((0,), (0,)), ((), ())),
+        right_hot, left_hot, (((1,), (1,)), ((), ())),
         precision=lax.Precision.HIGHEST, preferred_element_type=F32,
     )
     c_vec[...] = coupling[:nv]
@@ -163,8 +167,10 @@
 
         lax.fori_loop(0, nk // 2, terms, 0)
         for c in range(2 * CAP):
-            off_hi[q, c] = t_hi[picks[c]]
-            off_lo[q, c] = t_lo[picks[c]]
+            hi, lo = t_hi[picks[c]], t_lo[picks[c]]
+            for h in range(per):
+                off_hi[q * per + h, c] = hi[:, h * narrow:(h + 1) * narrow]
+                off_lo[q * per + h, c] = lo[:, h * narrow:(h + 1) * narrow]
 
         rhs = r_cat[pl.ds(q * vc, vc)].reshape(wide, 2 * bs)
 
@@ -180,41 +186,46 @@
 
     lax.fori_loop(0, nq, own, 0)
 
-    def away(q, carry):
-        at = pl.ds(q * vc, vc)
-
-        def add(came, first):
-            hi, lo = split(came[at].reshape(wide, bs))
-            rows = slice(first, first + CAP)
-            a = off_hi[q, rows].reshape(CAP * bs, wide)
-            b = off_lo[q, rows].reshape(CAP * bs, wide)
-            total = dot(a, hi) + dot(a, lo) + dot(b, hi)
-            acc[nk + first:nk + first + CAP] += total.reshape(CAP, bs, bs)
-
-        @pl.when(has_dn)
-        def _():
-            up_copy(q).wait_recv()
-            add(r_lo, CAP)
-
-        @pl.when(has_up)
-        def _():
-            dn_copy(q).wait_recv()
-            add(r_hi, 0)
-
-        return carry
-
-    lax.fori_loop(0, nq, away, 0)
+    def lines(x):
+        return jnp.sum(x.reshape(bs // 8, 8, bs), axis=0)
 
     s1 = jnp.zeros((8, bs), F32)
     s2 = jnp.zeros((8, bs), F32)
     for k in range(nk):
-        product = acc[slots[k]]
         block = psi[k]
-        hp[k] = product
-        s1 = s1 + jnp.sum((block * product).reshape(bs // 8, 8, bs), axis=0)
-        s2 = s2 + jnp.sum((block * block).reshape(bs // 8, 8, bs), axis=0)
-    part[0:8] = s1
-    part[8:16] = s2
+        s1 = s1 + jnp.where(slots[k] == k, lines(block * acc[k]), 0.0)
+        s2 = s2 + lines(block * block)
+
+    def away(q, carry):
+        at = pl.ds(q * xc, xc)
+
+        def add(came, first):
+            hi, lo = split(came[at].reshape(narrow, bs))
+            rows = slice(first, first + CAP)
+            a = off_hi[q, rows].reshape(CAP * bs, narrow)
+            b = off_lo[q, rows].reshape(CAP * bs, narrow)
+            total = dot(a, hi) + dot(a, lo) + dot(b, hi)
+            acc[nk + first:nk + first + CAP] += total.reshape(CAP, bs, bs)
+
+        @pl.when(from_dn)
+        def _():
+            up_copy(q).wait_recv()
+            add(r_lo, CAP)
+
+        @pl.when(from_up)
+        def _():
+            dn_copy(q).wait_recv()
+            add(r_hi, 0)
+
+        return carry
+
+    lax.fori_loop(0, nx, away, 0)
+
+    for c in range(CAP):
+        s1 = s1 + jnp.where(n_up > c, lines(psi[picks[c]] * acc[nk + c]), 0.0)
+        s1 = s1 + jnp.where(n_dn > c, lines(psi[picks[CAP + c]] * acc[nk + CAP + c]), 0.0)
+    part[0:4] = s1[0:4] + s1[4:8]
+    part[4:8] = s2[0:4] + s2[4:8]
 
     def part_copy(d):
         return pltpu.make_async_remote_copy(
@@ -228,6 +239,8 @@
         return carry
 
     lax.fori_loop(1, n, tell, 0)
+    for k in range(nk):
+        hp[k] = acc[slots[k]]
     hp_copy = pltpu.make_async_copy(hp, hpsi_out, local_sem.at[3])
     hp_copy.start()
 
@@ -236,18 +249,15 @@
         return total + parts[d]
 
     total = lax.fori_loop(1, n, hear, part[...])
-    energy = jnp.sum(total[0:8], keepdims=True) / jnp.sum(total[8:16], keepdims=True)
-    for k in range(nk):
-        res[k] = hp[k] - energy * psi[k]
-    res_copy = pltpu.make_async_copy(res, res_out, local_sem.at[4])
-    res_copy.start()
+    energy = jnp.sum(total[0:4], keepdims=True) / jnp.sum(total[4:8], keepdims=True)
+    energy_out[...] = jnp.broadcast_to(energy, (8, bs))
 
     def sent(d, carry):
         part_copy(d).wait_send()
         return carry
 
     lax.fori_loop(1, n, sent, 0)
-    for q in range(nq):
+    for q in range(nx):
         @pl.when(has_up)
         def _():
             up_copy(q).wait_send()
@@ -257,27 +267,33 @@
             dn_copy(q).wait_send()
 
     hp_copy.wait()
-    res_copy.wait()
+
+
+def finish(hp, psi, energy, hpsi_out, res_out):
+    x = hp[...]
+    hpsi_out[...] = x
+    res_out[...] = x - energy[0:1, :][None] * psi[...]
 
 
 def on_device(n, psi, left_env, right_env, right_sector, mpo_pairs, mpo_coef):
     nk, bs, _ = psi.shape
     nv = left_env.shape[1]
     vc = 8 if nv % 8 == 0 else nv
-    nq = nv // vc
+    xc = 4 if nv % 8 == 0 else nv
+    nx = nv // xc
     vmem = pltpu.VMEM
     dma = pltpu.SemaphoreType.DMA
     anywhere = pl.BlockSpec(memory_space=pl.ANY)
-    return pl.pallas_call(
-        functools.partial(kernel, n, vc),
-        out_shape=(jax.ShapeDtypeStruct(psi.shape, F32), jax.ShapeDtypeStruct(psi.shape, F32)),
+    product, energy = pl.pallas_call(
+        functools.partial(kernel, n, vc, xc),
+        out_shape=(jax.ShapeDtypeStruct(psi.shape, F32), jax.ShapeDtypeStruct((8, bs), F32)),
         in_specs=[
             anywhere, anywhere, anywhere,
             pl.BlockSpec(memory_space=pltpu.SMEM),
             pl.BlockSpec(memory_space=vmem),
             pl.BlockSpec(memory_space=vmem),
         ],
-        out_specs=(anywhere, anywhere),
+        out_specs=(anywhere, pl.BlockSpec(memory_space=vmem)),
         scratch_shapes=[
             vmem((nk, bs, bs), F32),
             vmem((nv, bs, bs), F32),
@@ -289,23 +305,31 @@
             vmem((nv, bs, 2 * bs), BF16),
             vmem((nk, bs, vc * bs), BF16),
             vmem((nk, bs, vc * bs), BF16),
-            vmem((nq, 2 * CAP, bs, vc * bs), BF16),
-            vmem((nq, 2 * CAP, bs, vc * bs), BF16),
+            vmem((nx, 2 * CAP, bs, xc * bs), BF16),
+            vmem((nx, 2 * CAP, bs, xc * bs), BF16),
             vmem((nk + 2 * CAP, bs, bs), F32),
-            vmem((nk, bs, bs), F32),
             vmem((nk, bs, bs), F32),
             vmem((nv, 128), F32),
             pltpu.SMEM((nv, 128), F32),
-            vmem((16, bs), F32),
-            vmem((n, 16, bs), F32),
+            vmem((8, bs), F32),
+            vmem((n, 8, bs), F32),
             dma((6,)),
-            dma((nq,)), dma((nq,)), dma((nq,)), dma((nq,)),
+            dma((nx,)), dma((nx,)), dma((nx,)), dma((nx,)),
             dma((n,)), dma((n,)),
         ],
         compiler_params=pltpu.CompilerParams(
             collective_id=0, has_side_effects=True, vmem_limit_bytes=56 * 1024 * 1024
         ),
-    )(psi, left_env, right_env, right_sector, mpo_pairs, mpo_coef[:, None])
+    )(psi, left_env, right_env, right_sector, mpo_pairs.T, mpo_coef[None, :])
+    step = nk // 4
+    blocks = pl.BlockSpec((step, bs, bs), lambda i: (i, 0, 0))
+    return pl.pallas_call(
+        finish,
+        grid=(nk // step,),
+        out_shape=(jax.ShapeDtypeStruct(psi.shape, F32), jax.ShapeDtypeStruct(psi.shape, F32)),
+        in_specs=[blocks, blocks, pl.BlockSpec((8, bs), lambda i: (0, 0))],
+        out_specs=(blocks, blocks),
+    )(product, psi, energy)
 
 
 def solution(mesh):

time: 67.9 us -> 64.2 us (0.946)
  local copies, waits for them, and re-layouts: 6.1 us -> 0 us
  Pallas kernels: 60.9 us -> 63.3 us
    unnamed x5 -> x0, local copies, waits for them, and re-layouts: 4.74 us -> none
    pallas_call x1 -> x2, Pallas kernels: 60.9 us -> 63.3 us  [the longest x1 59.6 us: on_device(): pl.pallas_call(functools.partial(kernel, n, vc, xc), out_shape=(jax.Shape...]
    broadcast_in_dim x1 -> x0, local copies, waits for them, and re-layouts: 1.36 us -> none  [on_device(): mpo_coef[:, None]]
where the time goes in v2:
time: 64.2 us; the launch traced here: 64 us
  Pallas kernels  63.3 us (99%)
    pallas_call x1, Pallas kernels, on_device(): pl.pallas_call(functools.partial(kernel, n, vc, xc), out_shape=(jax.Shape...  59.6 us
    pallas_call x1, Pallas kernels, on_device(): pl.pallas_call(finish, grid=(nk // step,), out_shape=(jax.ShapeDtypeStruc...  3.76 us

profile of v2, /device:TPU:0, one launch (start us, length us, event | category | flops | bytes accessed | tf_op | source)
XLA Modules:
  0.0 64.0 jit_solution(2448466400110973498)
XLA Ops:
  0.6 59.6 %shard_map.77 = (f32[16,128,128]{2,1,0:T(8,128)}, f32[8,128]{1,0:T(8,128)}) custom-call(f32[16,128,128]{2,1,0:T(8,128)} %psi.1, f32[1,32,128,128]{3,2,1,0:T(8,128)} %left_in.1, f32[1,32,128,128]{3,2,1,0:T(8,128)} %right_in.1, s32[16]{0:T(128)} %sector.1, s32[2,64]{1,0:T(2,128)} %bitcast.2, f32[1,64]{1,0:T(1,128)} %bitcast.3), custom_call_target="tpu_custom_call" | custom-call | tf_op jit(solution)/shard_map/pallas_call | solution.py:287
  60.2 3.8 %shard_map.78 = (f32[16,128,128]{2,1,0:T(8,128)}, f32[16,128,128]{2,1,0:T(8,128)}) custom-call(f32[16,128,128]{2,1,0:T(8,128)} %get-tuple-element.4.hp, f32[16,128,128]{2,1,0:T(8,128)} %psi.1, f32[8,128]{1,0:T(8,128)} %get-tuple-element.5.energy), custom_call_target="tpu_custom_call" | custom-call | tf_op jit(solution)/shard_map/pallas_call | solution.py:326

commit v3 on v2

--- a/solution.py
+++ b/solution.py
@@ -25,8 +25,8 @@
     psi_in, left_in, right_in, sector, pairs, coef,
     hpsi_out, energy_out,
     psi, left, right, r_hi, r_lo, m_cat, p_cat, r_cat, t_hi, t_lo, off_hi, off_lo,
-    acc, hp, c_vec, c_sm, part, parts,
-    local_sem, up_send, up_recv, dn_send, dn_recv, part_send, part_recv,
+    acc, hp, hold, c_cat, part, parts,
+    local_sem, hold_send, hold_recv, up_send, up_recv, dn_send, dn_recv, part_send, part_recv,
 ):
     nk, bs, _ = psi.shape
     nv = left.shape[0]
@@ -56,35 +56,66 @@
     lax.fori_loop(1, n, greet, 0)
     pl.semaphore_wait(barrier, n - 1)
 
-    def up_copy(q):
+    def send(src, dst, q, send_sem, recv_sem, to):
         at = pl.ds(q * xc, xc)
         return pltpu.make_async_remote_copy(
-            src_ref=right_in.at[0, at], dst_ref=r_lo.at[at],
-            send_sem=up_send.at[q], recv_sem=up_recv.at[q],
-            device_id={"sect": me + 1}, device_id_type=pl.DeviceIdType.MESH,
+            src_ref=src.at[at], dst_ref=dst.at[at],
+            send_sem=send_sem.at[q], recv_sem=recv_sem.at[q],
+            device_id={"sect": to}, device_id_type=pl.DeviceIdType.MESH,
         )
 
+    mine = right_in.at[0]
+
+    def up_copy(q):
+        return send(mine, r_lo, q, up_send, up_recv, me + 1)
+
     def dn_copy(q):
-        at = pl.ds(q * xc, xc)
-        return pltpu.make_async_remote_copy(
-            src_ref=right_in.at[0, at], dst_ref=r_hi.at[at],
-            send_sem=dn_send.at[q], recv_sem=dn_recv.at[q],
-            device_id={"sect": me - 1}, device_id_type=pl.DeviceIdType.MESH,
-        )
+        return send(mine, r_hi, q, dn_send, dn_recv, me - 1)
+
+    rows = n // 4 if n % 4 == 0 else 1
+    row, place = lax.div(me, 4), lax.rem(me, 4)
+    zero = jnp.int32(0)
+    by_up = lax.div(nx * (rows - 1 - row), rows) if rows > 1 else zero
+    by_dn = lax.div(nx * row, rows) if rows > 1 else zero
+    up_count = jnp.where(place == 3, by_up, 0)
+    dn_count = jnp.where(place == 0, by_dn, 0)
+    hand_up = jnp.where(place == 1, by_up, 0)
+    hand_dn = jnp.where(place == 2, by_dn, 0)
+
+    def forward(i):
+        @pl.when(i < hand_up)
+        def _():
+            q = nx - hand_up + i
+            send(mine, hold, q, up_send, hold_recv, lax.rem(me + 1, n)).wait_recv()
+            send(hold, r_lo, q, hold_send, up_recv, me + 3).start()
+
+        @pl.when(i < hand_dn)
+        def _():
+            q = nx - hand_dn + i
+            send(mine, hold, q, dn_send, hold_recv, lax.rem(me + 1, n)).wait_recv()
+            send(hold, r_hi, q, hold_send, dn_recv, me - 3).start()
 
     has_up = me < n - 1
     has_dn = me > 0
     from_up, from_dn = has_up, has_dn
+    for i in range(nx):
+        @pl.when(i < up_count)
+        def _():
+            send(mine, hold, nx - up_count + i, up_send, hold_recv, me - 2).start()
+
+        @pl.when(i < dn_count)
+        def _():
+            send(mine, hold, nx - dn_count + i, dn_send, hold_recv, me + 2).start()
+
     for q in range(nx):
-        @pl.when(has_up)
+        @pl.when(has_up & (q < nx - up_count))
         def _():
             up_copy(q).start()
 
-        @pl.when(has_dn)
+        @pl.when(has_dn & (q < nx - dn_count))
         def _():
             dn_copy(q).start()
 
-    zero = jnp.int32(0)
     picks = [zero] * (2 * CAP)
     n_up = zero
     n_dn = zero
@@ -100,33 +131,39 @@
         n_up = n_up + up.astype(jnp.int32)
         n_dn = n_dn + dn.astype(jnp.int32)
 
-    ids = lax.broadcasted_iota(jnp.int32, (128, pairs.shape[1]), 0)
+    size = 8 * nv
+    ids = lax.div(lax.broadcasted_iota(jnp.int32, (size, pairs.shape[1]), 0), 8)
     left_hot = (pairs[0:1, :] == ids).astype(F32)
     right_hot = jnp.where(pairs[1:2, :] == ids, coef[...], 0.0)
     coupling = lax.dot_general(
         right_hot, left_hot, (((1,), (1,)), ((), ())),
         precision=lax.Precision.HIGHEST, preferred_element_type=F32,
     )
-    c_vec[...] = coupling[:nv]
-    c_copy = pltpu.make_async_copy(c_vec, c_sm, local_sem.at[5])
-    c_copy.start()
-    c_copy.wait()
+    here = lax.rem(lax.broadcasted_iota(jnp.int32, (size, size), 0), 8)
+    there = lax.rem(lax.broadcasted_iota(jnp.int32, (size, size), 1), 8)
+    c_hi, c_lo = split(jnp.where(here == there, coupling, 0.0))
+    c_cat[0] = c_hi
+    c_cat[1] = c_lo
 
     acc[...] = jnp.zeros_like(acc)
 
     loads[0].wait()
 
-    def mix(u, carry):
-        total = c_sm[u, 0] * left[0]
-        for w in range(1, nv):
-            total = total + c_sm[u, w] * left[w]
-        hi, lo = split(total)
-        m_cat[u, :, 0:bs] = hi
-        m_cat[u, :, bs:2 * bs] = lo
-        m_cat[u, :, 2 * bs:] = hi
-        return carry
-
-    lax.fori_loop(0, nv, mix, 0)
+    def mix(g, carry):
+        at = pl.multiple_of(g * 16, 16)
+        strip = jnp.concatenate(
+            [left[:, pl.ds(at, 8), :].reshape(size, bs), left[:, pl.ds(at + 8, 8), :].reshape(size, bs)], axis=1
+        )
+        l_hi, l_lo = split(strip)
+        total = dot(c_cat[0], l_hi) + dot(c_cat[0], l_lo) + dot(c_cat[1], l_hi)
+        both = jnp.concatenate([total[:, :bs].reshape(nv, 8, bs), total[:, bs:].reshape(nv, 8, bs)], axis=1)
+        hi, lo = split(both)
+        m_cat[:, pl.ds(at, 16), 0:bs] = hi
+        m_cat[:, pl.ds(at, 16), bs:2 * bs] = lo
+        m_cat[:, pl.ds(at, 16), 2 * bs:] = hi
+        return carry
+
+    lax.fori_loop(0, bs // 16, mix, 0)
 
     loads[1].wait()
 
@@ -166,6 +203,7 @@
             return carry
 
         lax.fori_loop(0, nk // 2, terms, 0)
+        forward(q)
         for c in range(2 * CAP):
             hi, lo = t_hi[picks[c]], t_lo[picks[c]]
             for h in range(per):
@@ -185,6 +223,8 @@
         return carry
 
     lax.fori_loop(0, nq, own, 0)
+    for i in range(nq, nx):
+        forward(i)
 
     def lines(x):
         return jnp.sum(x.reshape(bs // 8, 8, bs), axis=0)
@@ -266,13 +306,38 @@
         def _():
             dn_copy(q).wait_send()
 
+    for q in range(nx):
+        @pl.when(q >= nx - hand_up - hand_dn)
+        def _():
+            send(hold, r_lo, q, hold_send, up_recv, lax.rem(me + 1, n)).wait_send()
+
     hp_copy.wait()
 
 
-def finish(hp, psi, energy, hpsi_out, res_out):
-    x = hp[...]
-    hpsi_out[...] = x
-    res_out[...] = x - energy[0:1, :][None] * psi[...]
+def finish(parts, hp_in, psi_in, energy, hpsi_out, res_out, hp, psi, res, in_sem, out_sem):
+    step = hp.shape[0] // parts
+    at = [pl.ds(i * step, step) for i in range(parts)]
+    loads = [
+        (pltpu.make_async_copy(hp_in.at[a], hp.at[a], in_sem.at[0, i]), pltpu.make_async_copy(psi_in.at[a], psi.at[a], in_sem.at[1, i]))
+        for i, a in enumerate(at)
+    ]
+    stores = [
+        (pltpu.make_async_copy(hp.at[a], hpsi_out.at[a], out_sem.at[0, i]), pltpu.make_async_copy(res.at[a], res_out.at[a], out_sem.at[1, i]))
+        for i, a in enumerate(at)
+    ]
+    for first, second in loads:
+        first.start()
+        second.start()
+    quotient = energy[0:1, :][None]
+    for i, a in enumerate(at):
+        loads[i][0].wait()
+        stores[i][0].start()
+        loads[i][1].wait()
+        res[a] = hp[a] - quotient * psi[a]
+        stores[i][1].start()
+    for first, second in stores:
+        first.wait()
+        second.wait()
 
 
 def on_device(n, psi, left_env, right_env, right_sector, mpo_pairs, mpo_coef):
@@ -309,26 +374,24 @@
             vmem((nx, 2 * CAP, bs, xc * bs), BF16),
             vmem((nk + 2 * CAP, bs, bs), F32),
             vmem((nk, bs, bs), F32),
-            vmem((nv, 128), F32),
-            pltpu.SMEM((nv, 128), F32),
+            vmem((nv, bs, bs), F32),
+            vmem((2, 8 * nv, 8 * nv), BF16),
             vmem((8, bs), F32),
             vmem((n, 8, bs), F32),
-            dma((6,)),
-            dma((nx,)), dma((nx,)), dma((nx,)), dma((nx,)),
+            dma((4,)),
+            dma((nx,)), dma((nx,)), dma((nx,)), dma((nx,)), dma((nx,)), dma((nx,)),
             dma((n,)), dma((n,)),
         ],
         compiler_params=pltpu.CompilerParams(
             collective_id=0, has_side_effects=True, vmem_limit_bytes=56 * 1024 * 1024
         ),
     )(psi, left_env, right_env, right_sector, mpo_pairs.T, mpo_coef[None, :])
-    step = nk // 4
-    blocks = pl.BlockSpec((step, bs, bs), lambda i: (i, 0, 0))
     return pl.pallas_call(
-        finish,
-        grid=(nk // step,),
+        functools.partial(finish, 4),
         out_shape=(jax.ShapeDtypeStruct(psi.shape, F32), jax.ShapeDtypeStruct(psi.shape, F32)),
-        in_specs=[blocks, blocks, pl.BlockSpec((8, bs), lambda i: (0, 0))],
-        out_specs=(blocks, blocks),
+        in_specs=[anywhere, anywhere, pl.BlockSpec(memory_space=vmem)],
+        out_specs=(anywhere, anywhere),
+        scratch_shapes=[vmem(psi.shape, F32), vmem(psi.shape, F32), vmem(psi.shape, F32), dma((2, 4)), dma((2, 4))],
     )(product, psi, energy)
 
 

time: 64.2 us -> 63.2 us (0.984)
  Pallas kernels: 63.3 us -> 62.4 us
    pallas_call x1, Pallas kernels: 3.76 us -> 3.09 us  [on_device(): pl.pallas_call(functools.partial(finish, 4), out_shape=(jax.ShapeDtypeStr...]
where the time goes in v3:
time: 63.2 us; the launch traced here: 63 us
  Pallas kernels  62.4 us (99%)
  between operations  0.64 us (1%)
    pallas_call x1, Pallas kernels, on_device(): pl.pallas_call(functools.partial(kernel, n, vc, xc), out_shape=(jax.Shape...  59.3 us
    pallas_call x1, Pallas kernels, on_device(): pl.pallas_call(functools.partial(finish, 4), out_shape=(jax.ShapeDtypeStr...  3.09 us

profile of v3, /device:TPU:0, one launch (start us, length us, event | category | flops | bytes accessed | tf_op | source)
XLA Modules:
  0.0 63.0 jit_solution(3051194903525578150)
XLA Ops:
  0.6 59.3 %shard_map.77 = (f32[16,128,128]{2,1,0:T(8,128)}, f32[8,128]{1,0:T(8,128)}) custom-call(f32[16,128,128]{2,1,0:T(8,128)} %psi_in.3, f32[1,32,128,128]{3,2,1,0:T(8,128)} %left_in.1, f32[1,32,128,128]{3,2,1,0:T(8,128)} %right_in.1, s32[16]{0:T(128)} %sector.1, s32[2,64]{1,0:T(2,128)} %bitcast.2, f32[1,64]{1,0:T(1,128)} %bitcast.3), custom_call_target="tpu_custom_call" | custom-call | tf_op jit(solution)/shard_map/pallas_call | solution.py:352
  59.9 3.1 %shard_map.78 = (f32[16,128,128]{2,1,0:T(8,128)}, f32[16,128,128]{2,1,0:T(8,128)}) custom-call(f32[16,128,128]{2,1,0:T(8,128)} %get-tuple-element.4.hp_in, f32[16,128,128]{2,1,0:T(8,128)} %psi_in.3, f32[8,128]{1,0:T(8,128)} %get-tuple-element.5.energy), custom_call_target="tpu_custom_call" | custom-call | tf_op jit(solution)/shard_map/pallas_call | solution.py:389
